TPU v7x, 512 devices: a whole 4x8x8 slice. The times are simulated.
512 devices in a mesh: dp: 32 (over z, x_hi, core), comp: 16 (over x_lo, y).
Axes of the slice: x: 4 (x_hi: 2, x_lo: 2; x = x_hi * 2 + x_lo), y: 8, z: 8, core: 2. Of those that a mesh axis runs over, the one named last changes fastest.
Arguments:
- embeddings: float32 [32768, 768], P('dp'), may hold values from -6 to 6
- comp_means: float32 [8192, 768], P(('comp', 'dp')), may hold values from -1.2 to 1.2
- comp_variances: float32 [8192, 768], P(('comp', 'dp')), may hold values from 0.8 to 1.25
- comp_mass: float32 [8192], P(('comp', 'dp')), may hold values from 0.3 to 3
Outputs:
- new_means: float32 [8192, 768], P(('comp', 'dp'))
- new_variances: float32 [8192, 768], P(('comp', 'dp'))
- new_mass: float32 [8192], P(('comp', 'dp'))
All inputs are finite; a program needn't handle non-finite values.
Results may differ from a plain program's by a relative error of at most 0.0003.
Values sent between devices are 32-bit elements; how exact they have to be, the bound alone decides.
A program may use at most 64 MiB of HBM per device.

v0:
```python
import jax
import jax.numpy as jnp
from jax import lax
from jax.sharding import PartitionSpec as P


def coefficients(comp_means, comp_variances, comp_mass):
    precision = 1.0 / comp_variances
    neg_half = -0.5 * precision
    mean_prec = comp_means * precision
    offset = jnp.log(comp_mass) - 0.5 * jnp.sum(
        jnp.log(comp_variances) + comp_means * mean_prec, axis=1
    )
    return (neg_half, mean_prec, offset)


def moments_of(responsibility, values):
    return lax.dot_general(
        responsibility,
        values,
        (((0,), (0,)), ((), ())),
        precision=lax.Precision.HIGHEST,
        preferred_element_type=jnp.float32,
    )


def per_device(embeddings, comp_means, comp_variances, comp_mass):
    highest = lax.Precision.HIGHEST
    squares = embeddings * embeddings
    piece_half, piece_prec, piece_offset = coefficients(
        lax.all_gather(comp_means, "dp", axis=0, tiled=True),
        lax.all_gather(comp_variances, "dp", axis=0, tiled=True),
        lax.all_gather(comp_mass, "dp", axis=0, tiled=True),
    )
    quad = jnp.dot(squares, piece_half.T, precision=highest, preferred_element_type=jnp.float32)
    linear = jnp.dot(
        embeddings, piece_prec.T, precision=highest, preferred_element_type=jnp.float32
    )
    scores = quad + linear + piece_offset[None, :]
    local_peak = jnp.max(scores, axis=1)
    row_peak = lax.pmax(local_peak, "comp")
    shifted = jnp.exp(scores - row_peak[:, None])
    row_total = lax.psum(jnp.sum(shifted, axis=1), "comp")
    responsibility = shifted / row_total[:, None]
    first_sums = moments_of(responsibility, embeddings)
    second_sums = moments_of(responsibility, squares)
    counts = jnp.sum(responsibility, axis=0)
    first_sums, second_sums, counts = (
        lax.psum_scatter(first_sums, "dp", scatter_dimension=0, tiled=True),
        lax.psum_scatter(second_sums, "dp", scatter_dimension=0, tiled=True),
        lax.psum_scatter(counts, "dp", scatter_dimension=0, tiled=True),
    )
    total_comps = comp_means.shape[0] * lax.axis_size("dp") * lax.axis_size("comp")
    total_rows = embeddings.shape[0] * lax.axis_size("dp")
    mass_scale = total_comps / total_rows
    new_mass = 0.4 * comp_mass + 0.6 * mass_scale * counts
    first_moment = 0.4 * comp_mass[:, None] * comp_means + 0.6 * mass_scale * first_sums
    second_moment = (
        0.4 * comp_mass[:, None] * (comp_variances + comp_means * comp_means)
        + 0.6 * mass_scale * second_sums
    )
    new_means = first_moment / new_mass[:, None]
    new_variances = second_moment / new_mass[:, None] - new_means * new_means
    return (new_means, new_variances, new_mass)


def solution(mesh):
    placed = (P("dp", None), P(("comp", "dp"), None), P(("comp", "dp"), None), P(("comp", "dp")))
    return jax.shard_map(
        per_device,
        mesh=mesh,
        in_specs=placed,
        out_specs=(P(("comp", "dp"), None), P(("comp", "dp"), None), P(("comp", "dp"))),
        check_vma=False,
    )
```

profile of v0, /device:TPU:8, one launch (start us, length us, event | category | flops | bytes accessed | tf_op | source)
XLA Modules:
  0.0 530.1 jit_solution(17203534192863885605)
XLA Ops:
  7.2 0.0 all-gather.3.cloned.1.call-start
  7.2 0.7 all-gather.3.cloned.1.call-update
  7.9 0.0 all-gather.5.cloned.1.call-start
  7.9 0.7 all-gather.5.cloned.1.call-update
  8.6 0.0 reduce-scatter.3.cloned.1.call-start
  8.7 1.4 fusion.21
  10.7 0.9 dynamic-update-slice
  11.6 76.0 %all-reduce = f32[512]{0:T(512)S(1)} all-reduce(f32[512]{0:T(512)S(1)} %dynamic-update-slice), channel_id=1, replica_groups=mesh['dp'=32,'comp'=16] {'dp'}, use_global_device_ids=true, to_apply=%add | all-reduce | flops 512 | bytes 4096
  87.6 13.2 %all-gather.3.cloned.1.call-done = f32[512,768]{1,0:T(8,128)} async-done(((f32[16,768]{1,0:T(8,128)}), f32[512,768]{1,0:T(8,128)}) %all-gather.3.cloned.1.call-update) | async-done | bytes 1572880 | tf_op jit(solution)/shard_map/all_gather | solution.py:32
  100.8 84.3 %all-gather.5.cloned.1.call-done = f32[512,768]{1,0:T(8,128)} async-done(((f32[16,768]{1,0:T(8,128)}), f32[512,768]{1,0:T(8,128)}) %all-gather.5.cloned.1.call-update) | async-done | bytes 1572880 | tf_op jit(solution)/shard_map/all_gather | solution.py:31
  185.1 2.6 add_reduce_fusion
  187.7 0.0 copy-done
  187.7 0.0 copy-done.2
  187.7 0.0 copy-start.1
  187.7 0.0 copy-start.3
  187.7 7.3 %fusion.10 = f32[512,1024]{1,0:T(8,128)S(1)} fusion(f32[1024,768]{1,0:T(8,128)} %param.4, f32[512,768]{1,0:T(8,128)S(1)} %copy-done.2, f32[512,768]{1,0:T(8,128)S(1)} %copy-done), kind=kOutput, calls=%fused_computation.11 | convolution fusion | flops 4832624640 | bytes 8388608 | tf_op jit(solution)/shard_map/dot_general | solution.py:36
  195.0 5.4 %fusion.22 = (f32[1024]{0:T(1024)S(1)}, f32[1024,512]{0,1:T(8,128)S(1)}) fusion(f32[512]{0:T(512)S(1)} %multiply_subtract_fusion.1, f32[512,1024]{1,0:T(8,128)S(1)} %fusion.10, f32[512,768]{1,0:T(8,128)S(1)} %copy-done.1, f32[1024,768]{1,0:T(8,128)S(1)} %copy-done.3), kind=kOutput, calls=%fused_computation.27 | convolution fusion | flops 4834982912 | bytes 8919040 | tf_op jit(solution)/shard_map/dot_general | solution.py:35
  200.4 31.3 %pmax.7 = f32[1024]{0:T(1024)S(1)} all-reduce(f32[1024]{0:T(1024)S(1)} %get-tuple-element.9), channel_id=1, replica_groups=mesh['dp'=32,'comp'=16] {'comp'}, use_global_device_ids=true, to_apply=%region_2.0 | all-reduce | flops 1024 | bytes 8192 | tf_op jit(solution)/shard_map/pmax | solution.py:41
  231.7 0.3 fusion.6
  232.1 33.5 %psum.7 = f32[1024]{0:T(1024)S(1)} all-reduce(f32[1024]{0:T(1024)S(1)} %fusion.6), channel_id=1, replica_groups=mesh['dp'=32,'comp'=16] {'comp'}, use_global_device_ids=true, to_apply=%region_4.0 | all-reduce | flops 1024 | bytes 8192 | tf_op jit(solution)/shard_map/psum | solution.py:43
  265.5 8.4 %fusion.19 = f32[512,768]{1,0:T(8,128)} fusion(f32[1024,768]{1,0:T(8,128)} %param.4, f32[1024,512]{0,1:T(8,128)S(1)} %get-tuple-element.10, f32[1024]{0:T(1024)S(1)} %psum.7, f32[1024]{0:T(1024)S(1)} %pmax.7), kind=kOutput, calls=%fused_computation.25 | convolution fusion | flops 4832886784 | bytes 6823936 | tf_op jit(solution)/shard_map/dot_general | solution.py:18
  274.0 0.0 reduce-scatter.3.cloned.1.call-update
  274.0 0.0 reduce-scatter.5.cloned.1.call-start
  274.0 8.5 %fusion = f32[512,768]{1,0:T(8,128)} fusion(f32[1024,768]{1,0:T(8,128)} %param.4, f32[1024,512]{0,1:T(8,128)S(1)} %get-tuple-element.10, f32[1024]{0:T(1024)S(1)} %psum.7, f32[1024]{0:T(1024)S(1)} %pmax.7), kind=kOutput, calls=%fused_computation | convolution fusion | flops 4833673216 | bytes 6823936 | tf_op jit(solution)/shard_map/dot_general | solution.py:18
  282.5 0.0 reduce-scatter.5.cloned.1.call-update
  283.2 0.4 fusion.18
  283.6 65.1 %all-reduce.1 = f32[512]{0:T(512)S(1)} all-reduce(f32[512]{0:T(512)S(1)} %fusion.18), channel_id=3, replica_groups=mesh['dp'=32,'comp'=16] {'dp'}, use_global_device_ids=true, to_apply=%region_7.0.clone | all-reduce | flops 512 | bytes 4096
  348.8 0.0 copy-done.7
  348.8 0.1 broadcast_multiply_fusion
  348.9 44.6 %reduce-scatter.3.cloned.1.call-done = f32[16,768]{1,0:T(8,128)} async-done(((f32[512,768]{1,0:T(8,128)}), f32[16,768]{1,0:T(8,128)}) %reduce-scatter.3.cloned.1.call-update) | async-done | bytes 49168 | tf_op jit(solution)/shard_map/reduce_scatter | solution.py:49
  393.5 128.5 %reduce-scatter.5.cloned.1.call-done = f32[16,768]{1,0:T(8,128)} async-done(((f32[512,768]{1,0:T(8,128)}), f32[16,768]{1,0:T(8,128)}) %reduce-scatter.5.cloned.1.call-update) | async-done | bytes 49168 | tf_op jit(solution)/shard_map/reduce_scatter | solution.py:50
  522.0 1.5 multiply_subtract_fusion
  (13 shorter events, 0.0 us)
Async XLA Ops:
  7.2 93.6 %all-gather.3.cloned.1.call-start = ((), (), s32[]{:S(2)}) async-start(), calls=%async_computation.2 | async-start | bytes 1622016 | tf_op jit(solution)/shard_map/all_gather | solution.py:32
  7.9 177.2 %all-gather.5.cloned.1.call-start = ((), (), s32[]{:S(2)}) async-start(), calls=%async_computation.3 | async-start | bytes 1622016 | tf_op jit(solution)/shard_map/all_gather | solution.py:31
  8.6 384.8 %reduce-scatter.3.cloned.1.call-start = ((), (), s32[]{:S(2)}) async-start(), calls=%async_computation.4 | async-start | bytes 1622016 | tf_op jit(solution)/shard_map/reduce_scatter | solution.py:49
  100.8 86.9 %copy-start = (f32[512,768]{1,0:T(8,128)S(1)}, f32[512,768]{1,0:T(8,128)}, u32[]{:S(2)}) copy-start(f32[512,768]{1,0:T(8,128)} %all-gather.3.cloned.1.call-done) | copy-start | bytes 4718596
  185.1 2.6 copy-start.2
  187.7 7.3 %copy-start.1 = (f32[512,768]{1,0:T(8,128)S(1)}, f32[512,768]{1,0:T(8,128)}, u32[]{:S(2)}) copy-start(f32[512,768]{1,0:T(8,128)} %all-gather.3.cloned.1.call-done) | copy-start | bytes 4718596
  187.7 7.3 %copy-start.3 = (f32[1024,768]{1,0:T(8,128)S(1)}, f32[1024,768]{1,0:T(8,128)}, u32[]{:S(2)}) copy-start(f32[1024,768]{1,0:T(8,128)} %param.4) | copy-start | bytes 9437188
  274.0 248.0 %reduce-scatter.5.cloned.1.call-start = ((), (), s32[]{:S(2)}) async-start(), calls=%async_computation.5 | async-start | bytes 1622016 | tf_op jit(solution)/shard_map/reduce_scatter | solution.py:50
  282.5 66.3 %copy-start.7 = (f32[16]{0:T(128)S(1)}, f32[16]{0:T(128)}, u32[]{:S(2)}) copy-start(f32[16]{0:T(128)} %param.7) | copy-start | bytes 196
  282.5 239.5 %copy-start.4 = (f32[16,768]{1,0:T(8,128)S(1)}, f32[16,768]{1,0:T(8,128)}, u32[]{:S(2)}) copy-start(f32[16,768]{1,0:T(8,128)} %param.6) | copy-start | bytes 147460
  282.5 239.5 %copy-start.5 = (f32[16,768]{1,0:T(8,128)S(1)}, f32[16,768]{1,0:T(8,128)}, u32[]{:S(2)}) copy-start(f32[16,768]{1,0:T(8,128)} %param.5) | copy-start | bytes 147460
  348.9 174.7 %copy-start.6 = (f32[16]{0:T(128)}, f32[16]{0:T(128)S(1)}, u32[]{:S(2)}) copy-start(f32[16]{0:T(128)S(1)} %get-tuple-element.8) | copy-start | bytes 196
Sparse Core Ops, SparseCore 0:
  11.4 89.3 all-gather.2
  104.2 80.8 all-gather.4
  274.1 119.3 reduce-scatter.2
  398.0 123.9 reduce-scatter.4
where the time goes:
time: 530 us
  waiting for transfers between devices  272 us (51%)
  blocking collectives  206 us (39%)
  matrix products  29.6 us (6%)
  between operations  15.2 us (3%)
    unnamed x2, blocking collectives  141 us
    reduce_scatter x1, waiting for transfers between devices, per_device(): lax.psum_scatter(second_sums, 'dp', scatter_dimension=0, tiled=True)  129 us
    all_gather x1, waiting for transfers between devices, per_device(): lax.all_gather(comp_means, 'dp', axis=0, tiled=True)  84.3 us
    reduce_scatter x1, waiting for transfers between devices, per_device(): lax.psum_scatter(first_sums, 'dp', scatter_dimension=0, tiled=True)  44.6 us
    psum x1, blocking collectives, per_device(): row_total = lax.psum(jnp.sum(shifted, axis=1), 'comp')  33.5 us
    pmax x1, blocking collectives, per_device(): row_peak = lax.pmax(local_peak, 'comp')  31.3 us
    dot_general x2, matrix products, moments_of(): lax.dot_general(responsibility, values, (((0,), (0,)), ((), ())), precisi...  16.9 us
    all_gather x1, waiting for transfers between devices, per_device(): lax.all_gather(comp_variances, 'dp', axis=0, tiled=True)  13.2 us
  transfers between devices with their start and end apart: 4, of which 4 were waited for; matrix products, arithmetic and copies ran while one was open for 2% of the time, Pallas kernels for 0%

commit v1 on v0

--- a/solution.py
+++ b/solution.py
@@ -28,7 +28,9 @@
     highest = lax.Precision.HIGHEST
     squares = embeddings * embeddings
     piece_half, piece_prec, piece_offset = coefficients(
-        lax.all_gather(comp_means, "dp", axis=0, tiled=True),
+        jnp.concatenate(
+            lax.all_to_all(jnp.stack([comp_means] * lax.axis_size("dp")), "dp", 0, 0), axis=0
+        ),
         lax.all_gather(comp_variances, "dp", axis=0, tiled=True),
         lax.all_gather(comp_mass, "dp", axis=0, tiled=True),
     )

time: 530 us -> 467 us (0.88)
  waiting for transfers between devices: 272 us -> 179 us
  blocking collectives: 206 us -> 224 us
  starting transfers between devices: 0.16 us -> 13.3 us
    all_gather x1 -> x0, waiting for transfers between devices: 84.3 us -> none  [per_device(): lax.all_gather(comp_means, 'dp', axis=0, tiled=True)]
    unnamed x2, blocking collectives: 141 us -> 159 us
    all_gather x1, waiting for transfers between devices: 13.2 us -> 0.01 us  [per_device(): lax.all_gather(comp_variances, 'dp', axis=0, tiled=True)]
    all_to_all x0 -> x1, starting transfers between devices: none -> 13.2 us  [per_device(): lax.all_to_all(jnp.stack([comp_means] * lax.axis_size('dp')), 'dp', 0, 0)]
  transfers between devices with their start and end apart: 4 -> 4, of which waited for: 4 -> 2; matrix products, arithmetic and copies ran while one was open for 2% -> 3% of each run, Pallas kernels for 0% -> 0%
where the time goes in v1:
time: 467 us
  blocking collectives  224 us (48%)
  waiting for transfers between devices  179 us (38%)
  matrix products  27.6 us (6%)
  between operations  15.2 us (3%)
  starting transfers between devices  13.3 us (3%)
  other arithmetic  4.69 us (1%)
    unnamed x2, blocking collectives  159 us
    reduce_scatter x1, waiting for transfers between devices, per_device(): lax.psum_scatter(second_sums, 'dp', scatter_dimension=0, tiled=True)  129 us
    reduce_scatter x1, waiting for transfers between devices, per_device(): lax.psum_scatter(first_sums, 'dp', scatter_dimension=0, tiled=True)  49.3 us
    psum x1, blocking collectives, per_device(): row_total = lax.psum(jnp.sum(shifted, axis=1), 'comp')  33.5 us
    pmax x1, blocking collectives, per_device(): row_peak = lax.pmax(local_peak, 'comp')  31.9 us
    dot_general x2, matrix products, moments_of(): lax.dot_general(responsibility, values, (((0,), (0,)), ((), ())), precisi...  16.9 us
    all_to_all x1, starting transfers between devices, per_device(): lax.all_to_all(jnp.stack([comp_means] * lax.axis_size('dp')), 'dp', 0, 0)  13.2 us
  transfers between devices with their start and end apart: 4, of which 2 were waited for; matrix products, arithmetic and copies ran while one was open for 3% of the time, Pallas kernels for 0%

profile of v1, /device:TPU:8, one launch (start us, length us, event | category | flops | bytes accessed | tf_op | source)
XLA Modules:
  0.0 466.8 jit_solution(10426564410813477094)
XLA Ops:
  7.2 0.0 all-gather.2.cloned.1.call-start
  7.2 0.7 all-gather.2.cloned.1.call-update
  7.9 0.0 copy-start.5
  7.9 0.0 copy-start.6
  7.9 2.1 stack.2
  10.1 13.2 %all-to-all-start = ((f32[32,16,768]{2,1,0:T(8,128)}), f32[32,16,768]{2,1,0:T(8,128)S(1)}, u32[]{:S(2)}, u32[]{:S(2)}) async-start(f32[32,16,768]{2,1,0:T(8,128)} %stack.2), calls=%async_computation | async-start | bytes 3145728 | tf_op jit(solution)/shard_map/all_to_all | solution.py:32
  23.2 0.0 reduce-scatter.3.cloned.1.call-start
  23.3 0.0 copy-done.5
  23.3 0.6 fusion.20
  24.5 0.0 copy-done.6
  24.6 0.2 dynamic-update-slice
  24.8 93.9 %all-reduce = f32[512]{0:T(512)S(1)} all-reduce(f32[512]{0:T(512)S(1)} %dynamic-update-slice), channel_id=1, replica_groups=mesh['dp'=32,'comp'=16] {'dp'}, use_global_device_ids=true, to_apply=%add | all-reduce | flops 512 | bytes 4096
  118.7 0.0 all-to-all-done
  118.7 0.0 copy-start
  118.7 2.3 fusion.10
  121.0 0.0 copy-done
  121.1 5.3 %fusion.22 = f32[512,1024]{1,0:T(8,128)S(1)} fusion(f32[512,768]{1,0:T(8,128)S(1)} %get-tuple-element.6, f32[1024,768]{1,0:T(8,128)S(1)} %copy-done), kind=kOutput, calls=%fused_computation.28 | convolution fusion | flops 4831838208 | bytes 6815744 | tf_op jit(solution)/shard_map/dot_general | solution.py:38
  126.3 5.4 %fusion.21 = (f32[1024]{0:T(1024)S(1)}, f32[1024,512]{0,1:T(8,128)S(1)}) fusion(f32[512]{0:T(512)S(1)} %multiply_subtract_fusion.1, f32[512,1024]{1,0:T(8,128)S(1)} %fusion.22, f32[512,768]{1,0:T(8,128)S(1)} %copy-done.1, f32[1024,768]{1,0:T(8,128)S(1)} %copy-done), kind=kOutput, calls=%fused_computation.27 | convolution fusion | flops 4834982912 | bytes 8919040 | tf_op jit(solution)/shard_map/dot_general | solution.py:37
  131.8 31.9 %pmax.7 = f32[1024]{0:T(1024)S(1)} all-reduce(f32[1024]{0:T(1024)S(1)} %get-tuple-element.11), channel_id=1, replica_groups=mesh['dp'=32,'comp'=16] {'comp'}, use_global_device_ids=true, to_apply=%region_2.0 | all-reduce | flops 1024 | bytes 8192 | tf_op jit(solution)/shard_map/pmax | solution.py:43
  163.7 0.3 fusion.6
  164.0 33.5 %psum.7 = f32[1024]{0:T(1024)S(1)} all-reduce(f32[1024]{0:T(1024)S(1)} %fusion.6), channel_id=1, replica_groups=mesh['dp'=32,'comp'=16] {'comp'}, use_global_device_ids=true, to_apply=%region_4.0 | all-reduce | flops 1024 | bytes 8192 | tf_op jit(solution)/shard_map/psum | solution.py:45
  197.5 8.4 %fusion.18 = f32[512,768]{1,0:T(8,128)} fusion(f32[1024,768]{1,0:T(8,128)} %param.4, f32[1024,512]{0,1:T(8,128)S(1)} %get-tuple-element.12, f32[1024]{0:T(1024)S(1)} %psum.7, f32[1024]{0:T(1024)S(1)} %pmax.7), kind=kOutput, calls=%fused_computation.25 | convolution fusion | flops 4832886784 | bytes 6823936 | tf_op jit(solution)/shard_map/dot_general | solution.py:18
  205.9 0.0 reduce-scatter.3.cloned.1.call-update
  206.0 0.0 reduce-scatter.5.cloned.1.call-start
  206.0 8.5 %fusion = f32[512,768]{1,0:T(8,128)} fusion(f32[1024,768]{1,0:T(8,128)} %param.4, f32[1024,512]{0,1:T(8,128)S(1)} %get-tuple-element.12, f32[1024]{0:T(1024)S(1)} %psum.7, f32[1024]{0:T(1024)S(1)} %pmax.7), kind=kOutput, calls=%fused_computation | convolution fusion | flops 4833673216 | bytes 6823936 | tf_op jit(solution)/shard_map/dot_general | solution.py:18
  214.5 0.0 reduce-scatter.5.cloned.1.call-update
  215.2 0.4 fusion.17
  215.6 65.1 %all-reduce.1 = f32[512]{0:T(512)S(1)} all-reduce(f32[512]{0:T(512)S(1)} %fusion.17), channel_id=3, replica_groups=mesh['dp'=32,'comp'=16] {'dp'}, use_global_device_ids=true, to_apply=%region_7.0.clone | all-reduce | flops 512 | bytes 4096
  280.7 0.1 broadcast_multiply_fusion
  280.8 49.3 %reduce-scatter.3.cloned.1.call-done = f32[16,768]{1,0:T(8,128)} async-done(((f32[512,768]{1,0:T(8,128)}), f32[16,768]{1,0:T(8,128)}) %reduce-scatter.3.cloned.1.call-update) | async-done | bytes 49168 | tf_op jit(solution)/shard_map/reduce_scatter | solution.py:51
  330.2 128.5 %reduce-scatter.5.cloned.1.call-done = f32[16,768]{1,0:T(8,128)} async-done(((f32[512,768]{1,0:T(8,128)}), f32[16,768]{1,0:T(8,128)}) %reduce-scatter.5.cloned.1.call-update) | async-done | bytes 49168 | tf_op jit(solution)/shard_map/reduce_scatter | solution.py:52
  458.7 1.5 multiply_subtract_fusion
  (11 shorter events, 0.0 us)
Async XLA Ops:
  7.2 111.5 %all-gather.2.cloned.1.call-start = ((), (), s32[]{:S(2)}) async-start(), calls=%async_computation.3 | async-start | bytes 1622016 | tf_op jit(solution)/shard_map/all_gather | solution.py:34
  7.9 15.4 %copy-start.5 = (u32[512]{0:T(512)S(1)}, u32[512]{0:T(512)}, u32[]{:S(2)}) copy-start(u32[512]{0:T(512)} %constant.21) | copy-start | bytes 6148
  7.9 16.6 %copy-start.6 = (f32[16]{0:T(128)S(1)}, f32[16]{0:T(128)}, u32[]{:S(2)}) copy-start(f32[16]{0:T(128)} %param.7) | copy-start | bytes 196
  10.1 108.6 %all-to-all-start = ((f32[32,16,768]{2,1,0:T(8,128)}), f32[32,16,768]{2,1,0:T(8,128)S(1)}, u32[]{:S(2)}, u32[]{:S(2)}) async-start(f32[32,16,768]{2,1,0:T(8,128)} %stack.2), calls=%async_computation | async-start | bytes 3145728 | tf_op jit(solution)/shard_map/all_to_all | solution.py:32
  23.2 306.9 %reduce-scatter.3.cloned.1.call-start = ((), (), s32[]{:S(2)}) async-start(), calls=%async_computation.4 | async-start | bytes 1622016 | tf_op jit(solution)/shard_map/reduce_scatter | solution.py:51
  118.7 2.4 copy-start
  121.1 5.3 %copy-start.1 = (f32[512,768]{1,0:T(8,128)S(1)}, f32[512,768]{1,0:T(8,128)}, u32[]{:S(2)}) copy-start(f32[512,768]{1,0:T(8,128)} %all-gather.2.cloned.1.call-done) | copy-start | bytes 4718596
  206.0 252.7 %reduce-scatter.5.cloned.1.call-start = ((), (), s32[]{:S(2)}) async-start(), calls=%async_computation.5 | async-start | bytes 1622016 | tf_op jit(solution)/shard_map/reduce_scatter | solution.py:52
  214.5 244.2 %copy-start.2 = (f32[16,768]{1,0:T(8,128)S(1)}, f32[16,768]{1,0:T(8,128)}, u32[]{:S(2)}) copy-start(f32[16,768]{1,0:T(8,128)} %param.5) | copy-start | bytes 147460
  214.5 244.2 %copy-start.3 = (f32[16,768]{1,0:T(8,128)S(1)}, f32[16,768]{1,0:T(8,128)}, u32[]{:S(2)}) copy-start(f32[16,768]{1,0:T(8,128)} %param.6) | copy-start | bytes 147460
  280.8 179.4 %copy-start.4 = (f32[16]{0:T(128)}, f32[16]{0:T(128)S(1)}, u32[]{:S(2)}) copy-start(f32[16]{0:T(128)S(1)} %get-tuple-element.10) | copy-start | bytes 196
Sparse Core Ops, SparseCore 0:
  11.4 94.6 all-gather.1
  206.1 124.0 reduce-scatter.2
  334.9 123.7 reduce-scatter.4
